TPU v7x, 512 devices: a whole 4x8x8 slice. The times are simulated.
512 devices in a mesh: band: 4 (over x_lo, core), shot: 16 (over x_hi, y), recv: 8 (over z).
Axes of the slice: x: 4 (x_hi: 2, x_lo: 2; x = x_hi * 2 + x_lo), y: 8, z: 8, core: 2. Of those that a mesh axis runs over, the one named last changes fastest.
Arguments:
- traces: float32 [1536, 384, 512], P(('band', 'shot'), 'recv'), parts along dimension 0, may hold values from -6 to 6
Outputs:
- predicted: float32 [1536, 384, 512], P(('band', 'shot'), 'recv'), parts along dimension 0
There are 4 independent parts, one for each index of `band`. A program takes and returns all parts, laid end to end along the dimension named above; each array names one. Nothing has to cross between parts.
All inputs are finite; a program needn't handle non-finite values.
Results may differ from a plain program's by a relative error of at most 0.000094.
Values sent between devices are 32-bit elements; how exact they have to be, the bound alone decides.
A program may use at most 64 MiB of HBM per device.

v0:
```python
import functools
import math

import jax
import jax.numpy as jnp
import numpy as np
from jax import lax
from jax.experimental import pallas as pl
from jax.experimental.pallas import tpu as pltpu
from jax.sharding import PartitionSpec as P

K0 = 32
NT = 512
NF = 64
SIZE = 384
SHOTS = 16
RECVS = 8
GROUP = SHOTS * RECVS
ROWS = SIZE // SHOTS
COLS = SIZE // RECVS
LANES = 128
PIECES = 9
F32 = jnp.float32
BF16 = jnp.bfloat16
MESH = pl.DeviceIdType.MESH


def split_np(table):
    high = table.astype(BF16)
    low = (table - high.astype(np.float32)).astype(BF16)
    return high, low


def tables():
    times = np.arange(NT)
    bins = np.arange(NF) + K0
    angles = (times[:, None] * bins[None, :] % NT) * (2.0 * math.pi / NT)
    cosines, sines = np.cos(angles), np.sin(angles)
    forward = np.concatenate([cosines, -sines], axis=1) / math.sqrt(NT * SIZE)
    inverse = np.concatenate([cosines.T, -sines.T], axis=0) * (2.0 * math.sqrt(SIZE / NT))
    f_high, f_low = split_np(forward.astype(np.float32))
    i_high, i_low = split_np(inverse.astype(np.float32))
    return np.concatenate([f_high, f_low], axis=1), np.concatenate([i_high, i_high, i_low], axis=0)


def split(value):
    high = value.astype(BF16)
    low = (value - high.astype(F32)).astype(BF16)
    return high, low


def dot(a, b):
    return jnp.dot(a, b, preferred_element_type=F32)


def exchange(regs):
    lane = lax.broadcasted_iota(jnp.int32, (8, LANES), 1)
    for bit in (1, 2, 4):
        upper = (lane & bit) != 0
        fresh = list(regs)
        for v in range(8):
            if v & bit:
                continue
            low, high = regs[v], regs[v | bit]
            fresh[v] = jnp.where(upper, pltpu.roll(high, bit, 1), low)
            fresh[v | bit] = jnp.where(upper, high, pltpu.roll(low, LANES - bit, 1))
        regs = fresh
    return regs


def owner_kernel(
    traces, table, back,
    tile, spec, stage, land, raw, sym, d_high, d_low, n_high, n_low, total, leave,
    load_sem, send_sem, recv_sem, own_sem, send2_sem, recv2_sem, own2_sem,
):
    band, shot, recv = lax.axis_index("band"), lax.axis_index("shot"), lax.axis_index("recv")
    parity = lax.rem(band, 2)
    me = shot * RECVS + recv
    is_owner = lax.rem(shot + recv + parity, 2) == 0
    my_bin = shot * 4 + recv // 2
    my_slot = (lax.rem(shot, 2) * 8 + recv) * 8 + shot // 2

    loads = []
    for third in range(3):
        part = pl.ds(third * 8, 8)
        loads.append(pltpu.make_async_copy(traces.at[part], tile.at[part], load_sem.at[third]))
        loads[-1].start()

    barrier = pltpu.get_barrier_semaphore()

    def greet(k, carry):
        other = lax.rem(me + k, GROUP)
        pl.semaphore_signal(
            barrier, inc=1, device_id=(band, other // RECVS, lax.rem(other, RECVS)), device_id_type=MESH
        )
        return carry

    lax.fori_loop(1, GROUP, greet, 0)

    for third in range(3):
        loads[third].wait()
        x_high, x_low = split(tile[pl.ds(third * 8, 8)].reshape(8 * COLS, NT))
        wide = dot(x_high, table[...])
        spec[...] = wide[:, :LANES] + wide[:, LANES:] + dot(x_low, table[:, :LANES])
        for c in range(3):
            rows = [spec[pl.ds(16 * c + m, 8, stride=COLS), :] for m in range(16)]
            turned = jnp.concatenate(rows, axis=0).T
            stage[third * 3 + c] = turned[:NF]
            stage[PIECES + third * 3 + c] = turned[NF:]

    pl.semaphore_wait(barrier, GROUP - 1)

    def send(k, carry):
        step = lax.rem(k * 29, NF)
        to_shot = lax.rem(shot + step // 4, SHOTS)
        to_quad = lax.rem(recv // 2 + step, 4)
        to_recv = 2 * to_quad + lax.rem(to_shot + parity, 2)
        source = stage.at[:, to_shot * 4 + to_quad, :]
        target = land.at[:, my_slot, :]
        mine = (to_shot == shot) & (to_recv == recv)

        @pl.when(mine)
        def _():
            pltpu.make_async_copy(source, target, own_sem).start()

        @pl.when(jnp.logical_not(mine))
        def _():
            pltpu.make_async_remote_copy(
                src_ref=source, dst_ref=target, send_sem=send_sem, recv_sem=recv_sem,
                device_id=(band, to_shot, to_recv), device_id_type=MESH,
            ).start()

        return carry

    lax.fori_loop(0, NF, send, 0)

    @pl.when(is_owner)
    def _():
        one = land.at[:, 0, :]
        pltpu.make_async_copy(one, one, own_sem).wait()
        rest = land.at[:, pl.ds(0, GROUP - 1), :]
        pltpu.make_async_copy(rest, rest, recv_sem).wait()

        for comp in range(2):
            def arrange(block, carry):
                half, third = block // 3, lax.rem(block, 3)
                for c in range(3):
                    regs = [
                        land[comp * PIECES + third * 3 + c, pl.ds(pl.multiple_of((half * 8 + v) * 8, 8), 8), :]
                        for v in range(8)
                    ]
                    regs = exchange(regs)
                    for v in range(8):
                        row = pl.multiple_of((half * 24 + third * 8 + v) * 8, 8)
                        raw[comp, pl.ds(row, 8), c * LANES:(c + 1) * LANES] = regs[v]
                return carry

            lax.fori_loop(0, 6, arrange, 0)

        for comp in range(2):
            for p in range(3):
                for q in range(3):
                    rows, cols = slice(p * LANES, (p + 1) * LANES), slice(q * LANES, (q + 1) * LANES)
                    value = 0.5 * (raw[comp, rows, cols] + raw[comp, cols, rows].T)
                    high, low = split(value)
                    here = slice(comp * SIZE + q * LANES, comp * SIZE + (q + 1) * LANES)
                    there = slice((1 - comp) * SIZE + q * LANES, (1 - comp) * SIZE + (q + 1) * LANES)
                    sym[rows, here] = value
                    d_high[rows, here] = high
                    d_low[rows, here] = low
                    n_high[rows, there] = high if comp == 0 else -high
                    n_low[rows, there] = low if comp == 0 else -low

        def product(high, low):
            out = dot(high[:, :SIZE], d_high[...]) + dot(high[:, SIZE:], n_high[...])
            out += dot(low[:, :SIZE], d_high[...]) + dot(low[:, SIZE:], n_high[...])
            return out + dot(high[:, :SIZE], d_low[...]) + dot(high[:, SIZE:], n_low[...])

        def half_of(half, carry):
            mine = pl.ds(pl.multiple_of(half * 192, 64), 192)
            square = product(d_high[mine, :], d_low[mine, :])
            s_high, s_low = split(square)
            total[...] = sym[mine, :] + square + product(s_high, s_low)

            def scatter(third, carry):
                for comp in range(2):
                    for c in range(3):
                        lanes = slice(comp * SIZE + c * LANES, comp * SIZE + (c + 1) * LANES)
                        regs = [total[pl.ds(pl.multiple_of((third * 8 + v) * 8, 8), 8), lanes] for v in range(8)]
                        regs = exchange(regs)
                        for v in range(8):
                            slot = pl.ds(pl.multiple_of((half * 8 + v) * 8, 8), 8)
                            leave[comp * PIECES + third * 3 + c, slot, :] = regs[v]
                return carry

            lax.fori_loop(0, 3, scatter, 0)

            def reply(k, carry):
                step = lax.rem(k * 29, 64)
                to_shot = lax.rem(shot // 2 + step // 8, 8) * 2 + half
                to_recv = lax.rem(recv + step, 8)
                slot = (half * 8 + to_recv) * 8 + to_shot // 2
                source = leave.at[:, slot, :]
                target = back.at[:, my_bin, :]
                mine = (to_shot == shot) & (to_recv == recv)

                @pl.when(mine)
                def _():
                    pltpu.make_async_copy(source, target, own2_sem).start()

                @pl.when(jnp.logical_not(mine))
                def _():
                    pltpu.make_async_remote_copy(
                        src_ref=source, dst_ref=target, send_sem=send2_sem, recv_sem=recv2_sem,
                        device_id=(band, to_shot, to_recv), device_id_type=MESH,
                    ).start()

                return carry

            lax.fori_loop(0, 64, reply, 0)
            return carry

        lax.fori_loop(0, 2, half_of, 0)

        pltpu.make_async_copy(stage.at[:, pl.ds(0, NF - 1), :], stage.at[:, pl.ds(0, NF - 1), :], send_sem).wait()
        one = back.at[:, 0, :]
        pltpu.make_async_copy(one, one, own2_sem).wait()
        rest = back.at[:, pl.ds(0, NF - 1), :]
        pltpu.make_async_copy(rest, rest, recv2_sem).wait()
        rest = leave.at[:, pl.ds(0, GROUP - 1), :]
        pltpu.make_async_copy(rest, rest, send2_sem).wait()

    @pl.when(jnp.logical_not(is_owner))
    def _():
        pltpu.make_async_copy(stage, stage, send_sem).wait()
        pltpu.make_async_copy(back, back, recv2_sem).wait()


def inverse_kernel(back, table, out, turned):
    third = pl.program_id(0)
    for c in range(3):
        both = jnp.concatenate([back[third * 3 + c], back[PIECES + third * 3 + c]], axis=0)
        turned[...] = both.T
        rows = [turned[pl.ds(a, 16, stride=8), :] for a in range(8)]
        high, low = split(jnp.concatenate(rows, axis=0))
        both = jnp.concatenate([high, low], axis=1)
        value = dot(both, table[:2 * LANES, :]) + dot(high, table[2 * LANES:, :])
        out[:, 16 * c:16 * (c + 1), :] = value.reshape(8, 16, NT)


def body(forward, inverse, traces):
    vmem = pl.BlockSpec(memory_space=pltpu.VMEM)
    back = pl.pallas_call(
        owner_kernel,
        out_shape=jax.ShapeDtypeStruct((2 * PIECES, NF, LANES), F32),
        in_specs=[pl.BlockSpec(memory_space=pl.ANY), vmem],
        out_specs=vmem,
        scratch_shapes=[
            pltpu.VMEM((ROWS, COLS, NT), F32),
            pltpu.VMEM((8 * COLS, LANES), F32),
            pltpu.VMEM((2 * PIECES, NF, LANES), F32),
            pltpu.VMEM((2 * PIECES, GROUP, LANES), F32),
            pltpu.VMEM((2, SIZE, SIZE), F32),
            pltpu.VMEM((SIZE, 2 * SIZE), F32),
            pltpu.VMEM((SIZE, 2 * SIZE), BF16),
            pltpu.VMEM((SIZE, 2 * SIZE), BF16),
            pltpu.VMEM((SIZE, 2 * SIZE), BF16),
            pltpu.VMEM((SIZE, 2 * SIZE), BF16),
            pltpu.VMEM((SIZE // 2, 2 * SIZE), F32),
            pltpu.VMEM((2 * PIECES, GROUP, LANES), F32),
            pltpu.SemaphoreType.DMA((3,)),
        ] + [pltpu.SemaphoreType.DMA] * 6,
        compiler_params=pltpu.CompilerParams(
            collective_id=0, has_side_effects=True, vmem_limit_bytes=40 * 2**20
        ),
    )(traces, forward)
    return pl.pallas_call(
        inverse_kernel,
        grid=(3,),
        out_shape=jax.ShapeDtypeStruct((ROWS, COLS, NT), F32),
        in_specs=[vmem, vmem],
        out_specs=pl.BlockSpec((8, COLS, NT), lambda third: (third, 0, 0)),
        scratch_shapes=[pltpu.VMEM((LANES, LANES), F32)],
        compiler_params=pltpu.CompilerParams(vmem_limit_bytes=20 * 2**20),
    )(back, inverse)


def solution(mesh):
    forward, inverse = tables()
    spec = P(("band", "shot"), "recv", None)
    return jax.shard_map(
        functools.partial(body, jnp.asarray(forward), jnp.asarray(inverse)),
        mesh=mesh, in_specs=(spec,), out_specs=spec, check_vma=False,
    )
```

profile of v0, /device:TPU:8, one launch (start us, length us, event | category | flops | bytes accessed | tf_op | source)
XLA Modules:
  0.0 73.9 jit_solution(2940296707731871315)
XLA Ops:
  0.0 0.0 copy-start
  0.0 1.7 %copy-done = f32[24,48,512]{2,1,0:T(8,128)S(1)} copy-done((f32[24,48,512]{2,1,0:T(8,128)S(1)}, f32[24,48,512]{2,1,0:T(8,128)}, u32[]{:S(2)}) %copy-start) | copy-done | bytes 2359320
  1.7 0.0 copy-start.2
  1.7 0.9 %copy-done.2 = bf16[512,256]{1,0:T(8,128)(2,1)S(1)} copy-done((bf16[512,256]{1,0:T(8,128)(2,1)S(1)}, bf16[512,256]{1,0:T(8,128)(2,1)}, u32[]{:S(2)}) %copy-start.2) | copy-done | bytes 262168
  2.6 0.0 copy-start.1
  2.6 68.6 %shard_map.37.back = f32[18,64,128]{2,1,0:T(8,128)S(1)} custom-call(f32[24,48,512]{2,1,0:T(8,128)S(1)} %copy-done, bf16[512,256]{1,0:T(8,128)(2,1)S(1)} %copy-done.2), custom_call_target="tpu_custom_call" | custom-call | tf_op jit(solution)/shard_map/pallas_call | solution.py:253
  71.2 0.0 copy-done.1
  71.2 2.7 %shard_map.38 = f32[24,48,512]{2,1,0:T(8,128)} custom-call(f32[18,64,128]{2,1,0:T(8,128)S(1)} %shard_map.37.back, bf16[384,512]{1,0:T(8,128)(2,1)S(1)} %copy-done.1), custom_call_target="tpu_custom_call" | custom-call | tf_op jit(solution)/shard_map/pallas_call | solution.py:277
Async XLA Ops:
  0.0 1.7 %copy-start = (f32[24,48,512]{2,1,0:T(8,128)S(1)}, f32[24,48,512]{2,1,0:T(8,128)}, u32[]{:S(2)}) copy-start(f32[24,48,512]{2,1,0:T(8,128)} %traces.1) | copy-start | bytes 7077892
  1.7 0.9 %copy-start.2 = (bf16[512,256]{1,0:T(8,128)(2,1)S(1)}, bf16[512,256]{1,0:T(8,128)(2,1)}, u32[]{:S(2)}) copy-start(bf16[512,256]{1,0:T(8,128)(2,1)} %constant.4.clone.table) | copy-start | bytes 786436
  2.6 68.6 %copy-start.1 = (bf16[384,512]{1,0:T(8,128)(2,1)S(1)}, bf16[384,512]{1,0:T(8,128)(2,1)}, u32[]{:S(2)}) copy-start(bf16[384,512]{1,0:T(8,128)(2,1)} %constant.5.clone.table) | copy-start | bytes 1179652
where the time goes:
time: 74.1 us; the launch traced here: 73.9 us
  Pallas kernels  71.3 us (96%)
  local copies, waits for them, and re-layouts  2.62 us (4%)
    pallas_call x1, Pallas kernels, body(): pl.pallas_call(owner_kernel, out_shape=jax.ShapeDtypeStruct((2 * PIECES,...  68.6 us
    pallas_call x1, Pallas kernels, body(): pl.pallas_call(inverse_kernel, grid=(3,), out_shape=jax.ShapeDtypeStruct(...  2.69 us
    unnamed x6, local copies, waits for them, and re-layouts  2.62 us

commit v1 on v0

--- a/solution.py
+++ b/solution.py
@@ -69,8 +69,8 @@
 
 
 def owner_kernel(
-    traces, table, back,
-    tile, spec, stage, land, raw, sym, d_high, d_low, n_high, n_low, total, leave,
+    traces, table_hbm, back,
+    tile, table, spec, stage, land, raw, sym, w_high, w_low, total, leave,
     load_sem, send_sem, recv_sem, own_sem, send2_sem, recv2_sem, own2_sem,
 ):
     band, shot, recv = lax.axis_index("band"), lax.axis_index("shot"), lax.axis_index("recv")
@@ -80,7 +80,8 @@
     my_bin = shot * 4 + recv // 2
     my_slot = (lax.rem(shot, 2) * 8 + recv) * 8 + shot // 2
 
-    loads = []
+    loads = [pltpu.make_async_copy(table_hbm, table, load_sem.at[3])]
+    loads[0].start()
     for third in range(3):
         part = pl.ds(third * 8, 8)
         loads.append(pltpu.make_async_copy(traces.at[part], tile.at[part], load_sem.at[third]))
@@ -97,8 +98,9 @@
 
     lax.fori_loop(1, GROUP, greet, 0)
 
+    loads[0].wait()
     for third in range(3):
-        loads[third].wait()
+        loads[third + 1].wait()
         x_high, x_low = split(tile[pl.ds(third * 8, 8)].reshape(8 * COLS, NT))
         wide = dot(x_high, table[...])
         spec[...] = wide[:, :LANES] + wide[:, LANES:] + dot(x_low, table[:, :LANES])
@@ -141,21 +143,19 @@
         rest = land.at[:, pl.ds(0, GROUP - 1), :]
         pltpu.make_async_copy(rest, rest, recv_sem).wait()
 
-        for comp in range(2):
-            def arrange(block, carry):
-                half, third = block // 3, lax.rem(block, 3)
+        def arrange(block, carry):
+            half, third = block // 3, lax.rem(block, 3)
+            for comp in range(2):
                 for c in range(3):
-                    regs = [
-                        land[comp * PIECES + third * 3 + c, pl.ds(pl.multiple_of((half * 8 + v) * 8, 8), 8), :]
-                        for v in range(8)
-                    ]
+                    piece = comp * PIECES + third * 3 + c
+                    regs = [land[piece, pl.ds(pl.multiple_of((half * 8 + v) * 8, 8), 8), :] for v in range(8)]
                     regs = exchange(regs)
                     for v in range(8):
                         row = pl.multiple_of((half * 24 + third * 8 + v) * 8, 8)
                         raw[comp, pl.ds(row, 8), c * LANES:(c + 1) * LANES] = regs[v]
-                return carry
-
-            lax.fori_loop(0, 6, arrange, 0)
+            return carry
+
+        lax.fori_loop(0, 6, arrange, 0)
 
         for comp in range(2):
             for p in range(3):
@@ -163,25 +163,25 @@
                     rows, cols = slice(p * LANES, (p + 1) * LANES), slice(q * LANES, (q + 1) * LANES)
                     value = 0.5 * (raw[comp, rows, cols] + raw[comp, cols, rows].T)
                     high, low = split(value)
+                    below = slice(SIZE + p * LANES, SIZE + (p + 1) * LANES)
                     here = slice(comp * SIZE + q * LANES, comp * SIZE + (q + 1) * LANES)
                     there = slice((1 - comp) * SIZE + q * LANES, (1 - comp) * SIZE + (q + 1) * LANES)
                     sym[rows, here] = value
-                    d_high[rows, here] = high
-                    d_low[rows, here] = low
-                    n_high[rows, there] = high if comp == 0 else -high
-                    n_low[rows, there] = low if comp == 0 else -low
+                    w_high[rows, here] = high
+                    w_low[rows, here] = low
+                    w_high[below, there] = high if comp == 0 else -high
+                    w_low[below, there] = low if comp == 0 else -low
 
         def product(high, low):
-            out = dot(high[:, :SIZE], d_high[...]) + dot(high[:, SIZE:], n_high[...])
-            out += dot(low[:, :SIZE], d_high[...]) + dot(low[:, SIZE:], n_high[...])
-            return out + dot(high[:, :SIZE], d_low[...]) + dot(high[:, SIZE:], n_low[...])
-
-        def half_of(half, carry):
+            both = dot(jnp.concatenate([high, low], axis=0), w_high[...])
+            return both[:SIZE // 2] + both[SIZE // 2:] + dot(high, w_low[...])
+
+        def half_of(turn, carry):
+            half = lax.rem(turn + recv, 2)
             mine = pl.ds(pl.multiple_of(half * 192, 64), 192)
-            square = product(d_high[mine, :], d_low[mine, :])
+            square = product(w_high[mine, :], w_low[mine, :])
             s_high, s_low = split(square)
             total[...] = sym[mine, :] + square + product(s_high, s_low)
-
             def scatter(third, carry):
                 for comp in range(2):
                     for c in range(3):
@@ -253,25 +253,24 @@
     back = pl.pallas_call(
         owner_kernel,
         out_shape=jax.ShapeDtypeStruct((2 * PIECES, NF, LANES), F32),
-        in_specs=[pl.BlockSpec(memory_space=pl.ANY), vmem],
+        in_specs=[pl.BlockSpec(memory_space=pl.ANY)] * 2,
         out_specs=vmem,
         scratch_shapes=[
             pltpu.VMEM((ROWS, COLS, NT), F32),
+            pltpu.VMEM((NT, 2 * LANES), BF16),
             pltpu.VMEM((8 * COLS, LANES), F32),
             pltpu.VMEM((2 * PIECES, NF, LANES), F32),
             pltpu.VMEM((2 * PIECES, GROUP, LANES), F32),
             pltpu.VMEM((2, SIZE, SIZE), F32),
             pltpu.VMEM((SIZE, 2 * SIZE), F32),
-            pltpu.VMEM((SIZE, 2 * SIZE), BF16),
-            pltpu.VMEM((SIZE, 2 * SIZE), BF16),
-            pltpu.VMEM((SIZE, 2 * SIZE), BF16),
-            pltpu.VMEM((SIZE, 2 * SIZE), BF16),
+            pltpu.VMEM((2 * SIZE, 2 * SIZE), BF16),
+            pltpu.VMEM((2 * SIZE, 2 * SIZE), BF16),
             pltpu.VMEM((SIZE // 2, 2 * SIZE), F32),
             pltpu.VMEM((2 * PIECES, GROUP, LANES), F32),
-            pltpu.SemaphoreType.DMA((3,)),
+            pltpu.SemaphoreType.DMA((4,)),
         ] + [pltpu.SemaphoreType.DMA] * 6,
         compiler_params=pltpu.CompilerParams(
-            collective_id=0, has_side_effects=True, vmem_limit_bytes=40 * 2**20
+            collective_id=0, has_side_effects=True, vmem_limit_bytes=53 * 2**20
         ),
     )(traces, forward)
     return pl.pallas_call(

time: 74.1 us -> 66.2 us (0.89)
  Pallas kernels: 71.3 us -> 65.1 us
  local copies, waits for them, and re-layouts: 2.62 us -> 1 us
    pallas_call x1, Pallas kernels: 68.6 us -> 62.4 us  [body(): pl.pallas_call(owner_kernel, out_shape=jax.ShapeDtypeStruct((2 * PIECES,...]
    unnamed x6 -> x4, local copies, waits for them, and re-layouts: 2.62 us -> 1 us
where the time goes in v1:
time: 66.2 us; the launch traced here: 66.1 us
  Pallas kernels  65.1 us (98%)
  local copies, waits for them, and re-layouts  1 us (2%)
    pallas_call x1, Pallas kernels, body(): pl.pallas_call(owner_kernel, out_shape=jax.ShapeDtypeStruct((2 * PIECES,...  62.4 us
    pallas_call x1, Pallas kernels, body(): pl.pallas_call(inverse_kernel, grid=(3,), out_shape=jax.ShapeDtypeStruct(...  2.69 us

profile of v1, /device:TPU:8, one launch (start us, length us, event | category | flops | bytes accessed | tf_op | source)
XLA Modules:
  0.0 66.1 jit_solution(14888659618061672147)
XLA Ops:
  0.0 0.0 copy-start
  0.0 0.0 copy-start.1
  0.0 1.0 %copy-done.1 = bf16[512,256]{1,0:T(8,128)(2,1)S(1)} copy-done((bf16[512,256]{1,0:T(8,128)(2,1)S(1)}, bf16[512,256]{1,0:T(8,128)(2,1)}, u32[]{:S(2)}) %copy-start.1) | copy-done | bytes 262168
  1.0 62.4 %shard_map.37.back = f32[18,64,128]{2,1,0:T(8,128)S(1)} custom-call(f32[24,48,512]{2,1,0:T(8,128)} %traces.1, bf16[512,256]{1,0:T(8,128)(2,1)S(1)} %copy-done.1), custom_call_target="tpu_custom_call" | custom-call | tf_op jit(solution)/shard_map/pallas_call | solution.py:253
  63.4 0.0 copy-done
  63.4 2.7 %shard_map.38 = f32[24,48,512]{2,1,0:T(8,128)} custom-call(f32[18,64,128]{2,1,0:T(8,128)S(1)} %shard_map.37.back, bf16[384,512]{1,0:T(8,128)(2,1)S(1)} %copy-done), custom_call_target="tpu_custom_call" | custom-call | tf_op jit(solution)/shard_map/pallas_call | solution.py:276
Async XLA Ops:
  0.0 63.4 %copy-start = (bf16[384,512]{1,0:T(8,128)(2,1)S(1)}, bf16[384,512]{1,0:T(8,128)(2,1)}, u32[]{:S(2)}) copy-start(bf16[384,512]{1,0:T(8,128)(2,1)} %constant.5.clone.table) | copy-start | bytes 1179652
  0.0 1.0 %copy-start.1 = (bf16[512,256]{1,0:T(8,128)(2,1)S(1)}, bf16[512,256]{1,0:T(8,128)(2,1)}, u32[]{:S(2)}) copy-start(bf16[512,256]{1,0:T(8,128)(2,1)} %constant.4.clone.table_hbm) | copy-start | bytes 786436

commit v2 on v1

--- a/solution.py
+++ b/solution.py
@@ -1,5 +1,6 @@
 import functools
 import math
+import random
 
 import jax
 import jax.numpy as jnp
@@ -25,6 +26,21 @@
 MESH = pl.DeviceIdType.MESH
 
 
+def ring(offset):
+    return min(offset, 8 - offset)
+
+
+def far_first(kept):
+    offsets = [(x, y, z) for x in range(2) for y in range(8) for z in range(8) if kept(x, y, z)]
+    random.Random(7).shuffle(offsets)
+    return sorted(offsets, key=lambda o: -(2 * o[0] + ring(o[1]) + ring(o[2])))
+
+
+GREET_ORDER = far_first(lambda x, y, z: True)[:-1]
+SEND_ORDER = [far_first(lambda x, y, z: (y + z) % 2 == odd) for odd in range(2)]
+REPLY_ORDER = [far_first(lambda x, y, z: y % 2 == odd) for odd in range(2)]
+
+
 def split_np(table):
     high = table.astype(BF16)
     low = (table - high.astype(np.float32)).astype(BF16)
@@ -75,7 +91,7 @@
 ):
     band, shot, recv = lax.axis_index("band"), lax.axis_index("shot"), lax.axis_index("recv")
     parity = lax.rem(band, 2)
-    me = shot * RECVS + recv
+    x_hi, y_at = shot // 8, lax.rem(shot, 8)
     is_owner = lax.rem(shot + recv + parity, 2) == 0
     my_bin = shot * 4 + recv // 2
     my_slot = (lax.rem(shot, 2) * 8 + recv) * 8 + shot // 2
@@ -89,14 +105,16 @@
 
     barrier = pltpu.get_barrier_semaphore()
 
-    def greet(k, carry):
-        other = lax.rem(me + k, GROUP)
-        pl.semaphore_signal(
-            barrier, inc=1, device_id=(band, other // RECVS, lax.rem(other, RECVS)), device_id_type=MESH
-        )
-        return carry
-
-    lax.fori_loop(1, GROUP, greet, 0)
+    def device(x, y, z):
+        return (lax.rem(x_hi + x, 2) * 8 + lax.rem(y_at + y, 8), lax.rem(recv + z, 8))
+
+    def pick(odd, orders, k):
+        even, uneven = orders[0][k], orders[1][k]
+        return [a if a == b else jnp.where(odd == 0, a, b) for a, b in zip(even, uneven)]
+
+    for offset in GREET_ORDER:
+        to_shot, to_recv = device(*offset)
+        pl.semaphore_signal(barrier, inc=1, device_id=(band, to_shot, to_recv), device_id_type=MESH)
 
     loads[0].wait()
     for third in range(3):
@@ -112,29 +130,24 @@
 
     pl.semaphore_wait(barrier, GROUP - 1)
 
-    def send(k, carry):
-        step = lax.rem(k * 29, NF)
-        to_shot = lax.rem(shot + step // 4, SHOTS)
-        to_quad = lax.rem(recv // 2 + step, 4)
-        to_recv = 2 * to_quad + lax.rem(to_shot + parity, 2)
-        source = stage.at[:, to_shot * 4 + to_quad, :]
-        target = land.at[:, my_slot, :]
-        mine = (to_shot == shot) & (to_recv == recv)
-
-        @pl.when(mine)
-        def _():
-            pltpu.make_async_copy(source, target, own_sem).start()
-
-        @pl.when(jnp.logical_not(mine))
-        def _():
-            pltpu.make_async_remote_copy(
-                src_ref=source, dst_ref=target, send_sem=send_sem, recv_sem=recv_sem,
-                device_id=(band, to_shot, to_recv), device_id_type=MESH,
-            ).start()
-
-        return carry
-
-    lax.fori_loop(0, NF, send, 0)
+    @pl.when(is_owner)
+    def _():
+        pltpu.make_async_copy(stage.at[:, my_bin, :], land.at[:, my_slot, :], own_sem).start()
+
+    def send(x, y, z):
+        to_shot, to_recv = device(x, y, z)
+        pltpu.make_async_remote_copy(
+            src_ref=stage.at[:, to_shot * 4 + to_recv // 2, :], dst_ref=land.at[:, my_slot, :],
+            send_sem=send_sem, recv_sem=recv_sem, device_id=(band, to_shot, to_recv), device_id_type=MESH,
+        ).start()
+
+    odd = lax.rem(shot + recv + parity, 2)
+    for k in range(NF - 1):
+        send(*pick(odd, SEND_ORDER, k))
+
+    @pl.when(jnp.logical_not(is_owner))
+    def _():
+        send(*SEND_ORDER[1][NF - 1])
 
     @pl.when(is_owner)
     def _():
@@ -195,29 +208,26 @@
 
             lax.fori_loop(0, 3, scatter, 0)
 
-            def reply(k, carry):
-                step = lax.rem(k * 29, 64)
-                to_shot = lax.rem(shot // 2 + step // 8, 8) * 2 + half
-                to_recv = lax.rem(recv + step, 8)
+            def reply(x, y, z):
+                to_shot, to_recv = device(x, y, z)
                 slot = (half * 8 + to_recv) * 8 + to_shot // 2
-                source = leave.at[:, slot, :]
-                target = back.at[:, my_bin, :]
-                mine = (to_shot == shot) & (to_recv == recv)
-
-                @pl.when(mine)
-                def _():
-                    pltpu.make_async_copy(source, target, own2_sem).start()
-
-                @pl.when(jnp.logical_not(mine))
-                def _():
-                    pltpu.make_async_remote_copy(
-                        src_ref=source, dst_ref=target, send_sem=send2_sem, recv_sem=recv2_sem,
-                        device_id=(band, to_shot, to_recv), device_id_type=MESH,
-                    ).start()
-
-                return carry
-
-            lax.fori_loop(0, 64, reply, 0)
+                pltpu.make_async_remote_copy(
+                    src_ref=leave.at[:, slot, :], dst_ref=back.at[:, my_bin, :],
+                    send_sem=send2_sem, recv_sem=recv2_sem, device_id=(band, to_shot, to_recv), device_id_type=MESH,
+                ).start()
+
+            apart = lax.rem(half + shot, 2)
+            for k in range(63):
+                reply(*pick(apart, REPLY_ORDER, k))
+
+            @pl.when(apart == 0)
+            def _():
+                pltpu.make_async_copy(leave.at[:, my_slot, :], back.at[:, my_bin, :], own2_sem).start()
+
+            @pl.when(apart == 1)
+            def _():
+                reply(*REPLY_ORDER[1][63])
+
             return carry
 
         lax.fori_loop(0, 2, half_of, 0)

time: 66.2 us -> 60.3 us (0.911)
  Pallas kernels: 65.1 us -> 58.9 us
    pallas_call x1, Pallas kernels: 62.4 us -> 56.3 us  [body(): pl.pallas_call(owner_kernel, out_shape=jax.ShapeDtypeStruct((2 * PIECES,...]
where the time goes in v2:
time: 60.3 us; the launch traced here: 60 us
  Pallas kernels  58.9 us (98%)
  local copies, waits for them, and re-layouts  1 us (2%)
    pallas_call x1, Pallas kernels, body(): pl.pallas_call(owner_kernel, out_shape=jax.ShapeDtypeStruct((2 * PIECES,...  56.3 us
    pallas_call x1, Pallas kernels, body(): pl.pallas_call(inverse_kernel, grid=(3,), out_shape=jax.ShapeDtypeStruct(...  2.69 us

profile of v2, /device:TPU:8, one launch (start us, length us, event | category | flops | bytes accessed | tf_op | source)
XLA Modules:
  0.0 60.0 jit_solution(9611782162031088799)
XLA Ops:
  0.0 0.0 copy-start
  0.0 0.0 copy-start.1
  0.0 1.0 %copy-done.1 = bf16[512,256]{1,0:T(8,128)(2,1)S(1)} copy-done((bf16[512,256]{1,0:T(8,128)(2,1)S(1)}, bf16[512,256]{1,0:T(8,128)(2,1)}, u32[]{:S(2)}) %copy-start.1) | copy-done | bytes 262168
  1.0 56.3 %shard_map.37.back = f32[18,64,128]{2,1,0:T(8,128)S(1)} custom-call(f32[24,48,512]{2,1,0:T(8,128)} %traces.1, bf16[512,256]{1,0:T(8,128)(2,1)S(1)} %copy-done.1), custom_call_target="tpu_custom_call" | custom-call | tf_op jit(solution)/shard_map/pallas_call | solution.py:263
  57.3 0.0 copy-done
  57.3 2.7 %shard_map.38 = f32[24,48,512]{2,1,0:T(8,128)} custom-call(f32[18,64,128]{2,1,0:T(8,128)S(1)} %shard_map.37.back, bf16[384,512]{1,0:T(8,128)(2,1)S(1)} %copy-done), custom_call_target="tpu_custom_call" | custom-call | tf_op jit(solution)/shard_map/pallas_call | solution.py:286
Async XLA Ops:
  0.0 57.3 %copy-start = (bf16[384,512]{1,0:T(8,128)(2,1)S(1)}, bf16[384,512]{1,0:T(8,128)(2,1)}, u32[]{:S(2)}) copy-start(bf16[384,512]{1,0:T(8,128)(2,1)} %constant.5.clone.table) | copy-start | bytes 1179652
  0.0 1.0 %copy-start.1 = (bf16[512,256]{1,0:T(8,128)(2,1)S(1)}, bf16[512,256]{1,0:T(8,128)(2,1)}, u32[]{:S(2)}) copy-start(bf16[512,256]{1,0:T(8,128)(2,1)} %constant.4.clone.table_hbm) | copy-start | bytes 786436

commit v3 on v2

--- a/solution.py
+++ b/solution.py
@@ -21,6 +21,7 @@
 COLS = SIZE // RECVS
 LANES = 128
 PIECES = 9
+TABLE_ROWS = 8192
 F32 = jnp.float32
 BF16 = jnp.bfloat16
 MESH = pl.DeviceIdType.MESH
@@ -56,7 +57,9 @@
     inverse = np.concatenate([cosines.T, -sines.T], axis=0) * (2.0 * math.sqrt(SIZE / NT))
     f_high, f_low = split_np(forward.astype(np.float32))
     i_high, i_low = split_np(inverse.astype(np.float32))
-    return np.concatenate([f_high, f_low], axis=1), np.concatenate([i_high, i_high, i_low], axis=0)
+    f_both = np.zeros((TABLE_ROWS, 2 * LANES), BF16)
+    f_both[:NT] = np.concatenate([f_high, f_low], axis=1)
+    return f_both, np.concatenate([i_high, i_high, i_low], axis=0)
 
 
 def split(value):
@@ -71,17 +74,11 @@
 
 def exchange(regs):
     lane = lax.broadcasted_iota(jnp.int32, (8, LANES), 1)
+    regs = [pltpu.roll(reg, v, 1) if v else reg for v, reg in enumerate(regs)]
     for bit in (1, 2, 4):
         upper = (lane & bit) != 0
-        fresh = list(regs)
-        for v in range(8):
-            if v & bit:
-                continue
-            low, high = regs[v], regs[v | bit]
-            fresh[v] = jnp.where(upper, pltpu.roll(high, bit, 1), low)
-            fresh[v | bit] = jnp.where(upper, high, pltpu.roll(low, LANES - bit, 1))
-        regs = fresh
-    return regs
+        regs = [jnp.where(upper, regs[(v + bit) % 8], regs[v]) for v in range(8)]
+    return [pltpu.roll(regs[8 - v], LANES - v, 1) if v else regs[0] for v in range(8)]
 
 
 def owner_kernel(
@@ -96,7 +93,7 @@
     my_bin = shot * 4 + recv // 2
     my_slot = (lax.rem(shot, 2) * 8 + recv) * 8 + shot // 2
 
-    loads = [pltpu.make_async_copy(table_hbm, table, load_sem.at[3])]
+    loads = [pltpu.make_async_copy(table_hbm.at[pl.ds(0, NT)], table, load_sem.at[3])]
     loads[0].start()
     for third in range(3):
         part = pl.ds(third * 8, 8)
@@ -246,16 +243,22 @@
         pltpu.make_async_copy(back, back, recv2_sem).wait()
 
 
-def inverse_kernel(back, table, out, turned):
-    third = pl.program_id(0)
-    for c in range(3):
-        both = jnp.concatenate([back[third * 3 + c], back[PIECES + third * 3 + c]], axis=0)
-        turned[...] = both.T
-        rows = [turned[pl.ds(a, 16, stride=8), :] for a in range(8)]
-        high, low = split(jnp.concatenate(rows, axis=0))
-        both = jnp.concatenate([high, low], axis=1)
-        value = dot(both, table[:2 * LANES, :]) + dot(high, table[2 * LANES:, :])
-        out[:, 16 * c:16 * (c + 1), :] = value.reshape(8, 16, NT)
+def inverse_kernel(back, table, out, turned, built, store_sem):
+    stores = []
+    for third in range(3):
+        for c in range(3):
+            piece = third * 3 + c
+            turned[piece] = jnp.concatenate([back[piece], back[PIECES + piece]], axis=0).T
+            rows = [turned[piece, pl.ds(a, 16, stride=8), :] for a in range(8)]
+            high, low = split(jnp.concatenate(rows, axis=0))
+            both = jnp.concatenate([high, low], axis=1)
+            value = dot(both, table[:2 * LANES, :]) + dot(high, table[2 * LANES:, :])
+            built[third * 8:(third + 1) * 8, 16 * c:16 * (c + 1), :] = value.reshape(8, 16, NT)
+        part = pl.ds(third * 8, 8)
+        stores.append(pltpu.make_async_copy(built.at[part], out.at[part], store_sem.at[third]))
+        stores[-1].start()
+    for store in stores:
+        store.wait()
 
 
 def body(forward, inverse, traces):
@@ -285,11 +288,14 @@
     )(traces, forward)
     return pl.pallas_call(
         inverse_kernel,
-        grid=(3,),
         out_shape=jax.ShapeDtypeStruct((ROWS, COLS, NT), F32),
         in_specs=[vmem, vmem],
-        out_specs=pl.BlockSpec((8, COLS, NT), lambda third: (third, 0, 0)),
-        scratch_shapes=[pltpu.VMEM((LANES, LANES), F32)],
+        out_specs=pl.BlockSpec(memory_space=pl.ANY),
+        scratch_shapes=[
+            pltpu.VMEM((PIECES, LANES, LANES), F32),
+            pltpu.VMEM((ROWS, COLS, NT), F32),
+            pltpu.SemaphoreType.DMA((3,)),
+        ],
         compiler_params=pltpu.CompilerParams(vmem_limit_bytes=20 * 2**20),
     )(back, inverse)
 

time: 60.3 us -> 57.8 us (0.959)
  Pallas kernels: 58.9 us -> 57.2 us
  local copies, waits for them, and re-layouts: 1 us -> 0.01 us
    unnamed x4 -> x2, local copies, waits for them, and re-layouts: 1 us -> 0.01 us
    pallas_call x1, Pallas kernels: 56.3 us -> 55.4 us  [body(): pl.pallas_call(owner_kernel, out_shape=jax.ShapeDtypeStruct((2 * PIECES,...]
    pallas_call x1, Pallas kernels: 2.69 us -> 1.89 us  [body(): pl.pallas_call(inverse_kernel, out_shape=jax.ShapeDtypeStruct((ROWS, COLS...]
where the time goes in v3:
time: 57.8 us; the launch traced here: 57.3 us
  Pallas kernels  57.2 us (99%)
    pallas_call x1, Pallas kernels, body(): pl.pallas_call(owner_kernel, out_shape=jax.ShapeDtypeStruct((2 * PIECES,...  55.4 us
    pallas_call x1, Pallas kernels, body(): pl.pallas_call(inverse_kernel, out_shape=jax.ShapeDtypeStruct((ROWS, COLS...  1.89 us

profile of v3, /device:TPU:8, one launch (start us, length us, event | category | flops | bytes accessed | tf_op | source)
XLA Modules:
  0.0 57.3 jit_solution(4887361920897544338)
XLA Ops:
  0.0 0.0 copy-start
  0.0 55.4 %shard_map.37.back = f32[18,64,128]{2,1,0:T(8,128)S(1)} custom-call(f32[24,48,512]{2,1,0:T(8,128)} %traces.1, bf16[8192,256]{1,0:T(8,128)(2,1)} %constant.4.clone.table_hbm), custom_call_target="tpu_custom_call" | custom-call | tf_op jit(solution)/shard_map/pallas_call | solution.py:266
  55.4 0.0 copy-done
  55.4 1.9 %shard_map.38 = f32[24,48,512]{2,1,0:T(8,128)} custom-call(f32[18,64,128]{2,1,0:T(8,128)S(1)} %shard_map.37.back, bf16[384,512]{1,0:T(8,128)(2,1)S(1)} %copy-done), custom_call_target="tpu_custom_call" | custom-call | tf_op jit(solution)/shard_map/pallas_call | solution.py:289
Async XLA Ops:
  0.0 55.4 %copy-start = (bf16[384,512]{1,0:T(8,128)(2,1)S(1)}, bf16[384,512]{1,0:T(8,128)(2,1)}, u32[]{:S(2)}) copy-start(bf16[384,512]{1,0:T(8,128)(2,1)} %constant.5.clone.table) | copy-start | bytes 1179652

commit v4 on v3

--- a/solution.py
+++ b/solution.py
@@ -135,7 +135,7 @@
         to_shot, to_recv = device(x, y, z)
         pltpu.make_async_remote_copy(
             src_ref=stage.at[:, to_shot * 4 + to_recv // 2, :], dst_ref=land.at[:, my_slot, :],
-            send_sem=send_sem, recv_sem=recv_sem, device_id=(band, to_shot, to_recv), device_id_type=MESH,
+            send_sem=send_sem, recv_sem=recv_sem.at[lax.rem(shot, 2)], device_id=(band, to_shot, to_recv), device_id_type=MESH,
         ).start()
 
     odd = lax.rem(shot + recv + parity, 2)
@@ -150,11 +150,18 @@
     def _():
         one = land.at[:, 0, :]
         pltpu.make_async_copy(one, one, own_sem).wait()
-        rest = land.at[:, pl.ds(0, GROUP - 1), :]
-        pltpu.make_async_copy(rest, rest, recv_sem).wait()
+
+        def arrived(half):
+            for count in (NF - 1, NF):
+                @pl.when((lax.rem(shot, 2) == half) == (count < NF))
+                def _():
+                    rest = land.at[:, pl.ds(half * NF, count), :]
+                    pltpu.make_async_copy(rest, rest, recv_sem.at[half]).wait()
+
+        arrived(1)
 
         def arrange(block, carry):
-            half, third = block // 3, lax.rem(block, 3)
+            half, third = 1 - block // 3, lax.rem(block, 3)
             for comp in range(2):
                 for c in range(3):
                     piece = comp * PIECES + third * 3 + c
@@ -165,7 +172,9 @@
                         raw[comp, pl.ds(row, 8), c * LANES:(c + 1) * LANES] = regs[v]
             return carry
 
-        lax.fori_loop(0, 6, arrange, 0)
+        lax.fori_loop(0, 3, arrange, 0)
+        arrived(0)
+        lax.fori_loop(3, 6, arrange, 0)
 
         for comp in range(2):
             for p in range(3):
@@ -281,7 +290,9 @@
             pltpu.VMEM((SIZE // 2, 2 * SIZE), F32),
             pltpu.VMEM((2 * PIECES, GROUP, LANES), F32),
             pltpu.SemaphoreType.DMA((4,)),
-        ] + [pltpu.SemaphoreType.DMA] * 6,
+            pltpu.SemaphoreType.DMA,
+            pltpu.SemaphoreType.DMA((2,)),
+        ] + [pltpu.SemaphoreType.DMA] * 4,
         compiler_params=pltpu.CompilerParams(
             collective_id=0, has_side_effects=True, vmem_limit_bytes=53 * 2**20
         ),

time: 57.8 us -> 57.3 us (level)
  the two profiles are of different devices: /device:TPU:8 before, /device:TPU:2 now
where the time goes in v4:
time: 57.3 us; the launch traced here: 57.2 us
  Pallas kernels  57.2 us (100%)
    pallas_call x1, Pallas kernels, body(): pl.pallas_call(owner_kernel, out_shape=jax.ShapeDtypeStruct((2 * PIECES,...  55.3 us
    pallas_call x1, Pallas kernels, body(): pl.pallas_call(inverse_kernel, out_shape=jax.ShapeDtypeStruct((ROWS, COLS...  1.89 us

profile of v4, /device:TPU:2, one launch (start us, length us, event | category | flops | bytes accessed | tf_op | source)
XLA Modules:
  0.0 57.2 jit_solution(5605960771595464633)
XLA Ops:
  0.0 0.0 copy-start
  0.0 55.3 %shard_map.37.back = f32[18,64,128]{2,1,0:T(8,128)S(1)} custom-call(f32[24,48,512]{2,1,0:T(8,128)} %traces.1, bf16[8192,256]{1,0:T(8,128)(2,1)} %constant.4.clone.table_hbm), custom_call_target="tpu_custom_call" | custom-call | tf_op jit(solution)/shard_map/pallas_call | solution.py:275
  55.3 0.0 copy-done
  55.3 1.9 %shard_map.38 = f32[24,48,512]{2,1,0:T(8,128)} custom-call(f32[18,64,128]{2,1,0:T(8,128)S(1)} %shard_map.37.back, bf16[384,512]{1,0:T(8,128)(2,1)S(1)} %copy-done), custom_call_target="tpu_custom_call" | custom-call | tf_op jit(solution)/shard_map/pallas_call | solution.py:300
Async XLA Ops:
  0.0 55.3 %copy-start = (bf16[384,512]{1,0:T(8,128)(2,1)S(1)}, bf16[384,512]{1,0:T(8,128)(2,1)}, u32[]{:S(2)}) copy-start(bf16[384,512]{1,0:T(8,128)(2,1)} %constant.5.clone.table) | copy-start | bytes 1179652

commit v5 on v4

--- a/solution.py
+++ b/solution.py
@@ -263,9 +263,9 @@
             both = jnp.concatenate([high, low], axis=1)
             value = dot(both, table[:2 * LANES, :]) + dot(high, table[2 * LANES:, :])
             built[third * 8:(third + 1) * 8, 16 * c:16 * (c + 1), :] = value.reshape(8, 16, NT)
-        part = pl.ds(third * 8, 8)
-        stores.append(pltpu.make_async_copy(built.at[part], out.at[part], store_sem.at[third]))
-        stores[-1].start()
+            part = (pl.ds(third * 8, 8), pl.ds(16 * c, 16))
+            stores.append(pltpu.make_async_copy(built.at[part], out.at[part], store_sem.at[piece]))
+            stores[-1].start()
     for store in stores:
         store.wait()
 
@@ -305,7 +305,7 @@
         scratch_shapes=[
             pltpu.VMEM((PIECES, LANES, LANES), F32),
             pltpu.VMEM((ROWS, COLS, NT), F32),
-            pltpu.SemaphoreType.DMA((3,)),
+            pltpu.SemaphoreType.DMA((PIECES,)),
         ],
         compiler_params=pltpu.CompilerParams(vmem_limit_bytes=20 * 2**20),
     )(back, inverse)

time: 57.3 us -> 57.2 us (level)
  no operation moved by 1% of the time
where the time goes in v5:
time: 57.2 us; the launch traced here: 57.1 us
  Pallas kernels  57.1 us (100%)
    pallas_call x1, Pallas kernels, body(): pl.pallas_call(owner_kernel, out_shape=jax.ShapeDtypeStruct((2 * PIECES,...  55.3 us
    pallas_call x1, Pallas kernels, body(): pl.pallas_call(inverse_kernel, out_shape=jax.ShapeDtypeStruct((ROWS, COLS...  1.8 us

profile of v5, /device:TPU:2, one launch (start us, length us, event | category | flops | bytes accessed | tf_op | source)
XLA Modules:
  0.0 57.1 jit_solution(6116706217397160909)
XLA Ops:
  0.0 0.0 copy-start
  0.0 55.3 %shard_map.37.back = f32[18,64,128]{2,1,0:T(8,128)S(1)} custom-call(f32[24,48,512]{2,1,0:T(8,128)} %traces.1, bf16[8192,256]{1,0:T(8,128)(2,1)} %constant.4.clone.table_hbm), custom_call_target="tpu_custom_call" | custom-call | tf_op jit(solution)/shard_map/pallas_call | solution.py:275
  55.3 0.0 copy-done
  55.3 1.8 %shard_map.38 = f32[24,48,512]{2,1,0:T(8,128)} custom-call(f32[18,64,128]{2,1,0:T(8,128)S(1)} %shard_map.37.back, bf16[384,512]{1,0:T(8,128)(2,1)S(1)} %copy-done), custom_call_target="tpu_custom_call" | custom-call | tf_op jit(solution)/shard_map/pallas_call | solution.py:300
Async XLA Ops:
  0.0 55.3 %copy-start = (bf16[384,512]{1,0:T(8,128)(2,1)S(1)}, bf16[384,512]{1,0:T(8,128)(2,1)}, u32[]{:S(2)}) copy-start(bf16[384,512]{1,0:T(8,128)(2,1)} %constant.5.clone.table) | copy-start | bytes 1179652
